TPU v7x, 32 devices: a whole 2x2x4 slice. The times are simulated.
32 devices in a mesh: groups: 2 (over x), rows: 16 (over z, y, core).
Axes of the slice: x: 2, y: 2, z: 4, core: 2. Of those that a mesh axis runs over, the one named last changes fastest.
Arguments:
- embeddings: bfloat16 [49152, 1024], P(('groups', 'rows')), parts along dimension 0
- block_cluster: int32 [384], P('groups'), parts along dimension 0, may hold values from 0 to 191, as said below
- pair_blocks: int32 [6720, 2], P(('groups', 'rows')), parts along dimension 0, may hold values from 0 to 191, as said below
Outputs:
- best_match: float32 [49152], P(('groups', 'rows')), parts along dimension 0
There are 2 independent parts, one for each index of `groups`. A program takes and returns all parts, laid end to end along the dimension named above; each array names one. Nothing has to cross between parts.
Inputs may be any that keep to these rules, and one draw needn't show every extreme that they name: `block_cluster`: every cluster is a run of consecutive blocks, at most 24 long; different clusters have different ids. `pair_blocks`: slots 210 * i to 210 * i + 209 belong to device i of rows. Each slot (a, b) has block a on that device and a <= b; the slots with a < b name each pair a < b of same-cluster blocks whose a lies on that device exactly once; the other slots have a == b.
All inputs are finite; a program needn't handle non-finite values.
Results may differ from a plain program's by a relative error of at most 0.0011.
Values may be sent and summed in bfloat16 or wider, within the bound.
No kernel may reach another device: no remote copies, remote signals or barrier semaphores. Data moves between devices by JAX's collectives and lax.ppermute only.
A program may use at most 64 MiB of HBM per device.

v0:
```python
import jax
import jax.numpy as jnp
from jax import lax
from jax.sharding import PartitionSpec as P

BLOCK = 128
LMAX = 24
REACH = 2


def shifted(block, axis, distance):
    devices = range(lax.axis_size(axis))
    route = [(i - distance, i) for i in devices if i - distance in devices]
    return lax.ppermute(block, axis, route)


def on_device(embeddings, block_cluster, pair_blocks):
    features = embeddings.shape[1]
    blocks_here = embeddings.shape[0] // BLOCK
    broadened_rows = embeddings.astype(jnp.float32)
    unit_rows = (
        broadened_rows
        * lax.rsqrt(jnp.sum(broadened_rows * broadened_rows, axis=1, keepdims=True) + 1e-06)
    ).astype(jnp.bfloat16)
    resident_blocks = unit_rows.reshape(blocks_here, BLOCK, features)
    first_block = lax.axis_index("rows") * blocks_here
    forward_block_count = LMAX - 1
    piece_sizes = [
        min(blocks_here, forward_block_count - offset * blocks_here) for offset in range(REACH)
    ]
    pieces = [resident_blocks]
    for offset, piece_size in enumerate(piece_sizes):
        pieces.append(shifted(resident_blocks[:piece_size], "rows", -(offset + 1)))
    block_pool = jnp.concatenate(pieces, axis=0)
    pool_count = blocks_here + forward_block_count
    left_rel = pair_blocks[:, 0] - first_block
    block_gap = pair_blocks[:, 1] - pair_blocks[:, 0]
    slot_code = jnp.where(block_gap > 0, left_rel * LMAX + block_gap, -1)
    enumerated_blocks = jnp.any(
        slot_code[:, None] == jnp.arange(blocks_here * LMAX, dtype=jnp.int32)[None, :], axis=0
    )
    enumerated_blocks = enumerated_blocks.reshape(blocks_here, LMAX)[:, 1:]
    padded_cluster = jnp.concatenate(
        [block_cluster, jnp.full((forward_block_count,), -1, jnp.int32)]
    )
    pool_cluster = lax.dynamic_slice_in_dim(padded_cluster, first_block, pool_count)
    ahead_cluster = jnp.stack(
        [pool_cluster[offset : offset + blocks_here] for offset in range(1, LMAX)], axis=1
    )
    counted = enumerated_blocks & (ahead_cluster == pool_cluster[:blocks_here, None])

    def band_step(turn_index, carry):
        row_best, running = carry
        companion_row = lax.dynamic_slice_in_dim(block_pool, turn_index + 1, blocks_here, 0)
        products = jnp.einsum(
            "hic,hjc->hij", resident_blocks, companion_row, preferred_element_type=jnp.float32
        )
        keep_tile = lax.dynamic_slice_in_dim(counted, turn_index, 1, 1)
        masked = jnp.where(keep_tile[:, :, None], products, jnp.float32(-3.0))
        row_best = jnp.maximum(row_best, jnp.max(masked, axis=2))
        current = lax.dynamic_slice_in_dim(running, turn_index + 1, blocks_here, 0)
        running = lax.dynamic_update_slice_in_dim(
            running, jnp.maximum(current, jnp.max(masked, axis=1)), turn_index + 1, 0
        )
        return (row_best, running)

    row_best = jnp.full((blocks_here, BLOCK), -3.0, jnp.float32)
    running = jnp.full((pool_count, BLOCK), -3.0, jnp.float32)
    row_best, running = lax.fori_loop(0, forward_block_count, band_step, (row_best, running))
    products = jnp.einsum(
        "hic,hjc->hij", resident_blocks, resident_blocks, preferred_element_type=jnp.float32
    )
    diagonal_mask = jnp.eye(BLOCK, dtype=bool)[None, :, :]
    own_best = jnp.max(jnp.where(diagonal_mask, jnp.float32(-3.0), products), axis=2)
    best_here = jnp.maximum(jnp.maximum(own_best, row_best), running[:blocks_here])
    devices = lax.axis_size("rows")
    everything = jnp.full((devices * blocks_here + forward_block_count, BLOCK), -3.0, jnp.float32)
    everything = lax.dynamic_update_slice_in_dim(
        everything, running[blocks_here:], first_block + blocks_here, 0
    )
    combined = lax.pmax(everything, "rows")
    best_here = jnp.maximum(
        best_here, lax.dynamic_slice_in_dim(combined, first_block, blocks_here, 0)
    )
    return best_here.reshape(-1)


def solution(mesh):
    placed = (P(("groups", "rows"), None), P("groups"), P(("groups", "rows"), None))
    return jax.shard_map(
        on_device, mesh=mesh, in_specs=placed, out_specs=P(("groups", "rows")), check_vma=False
    )
```

profile of v0, /device:TPU:8, one launch (start us, length us, event | category | flops | bytes accessed | tf_op | source)
XLA Modules:
  0.0 290.1 jit_solution(5548445068598918847)
XLA Ops:
  6.5 2.7 fusion.6
  9.4 0.6 fusion.7
  10.0 2.8 collective-permute-start
  12.7 1.8 slice.126
  14.6 2.5 collective-permute-start.1
  17.3 0.1 copy.33
  19.0 0.1 copy.28
  19.5 0.2 fusion.9
  19.8 0.1 stack.95
  20.0 0.1 copy.51
  20.1 90.4 %collective-permute-done.1 = bf16[11,128,1024]{2,1,0:T(8,128)(2,1)} collective-permute-done((bf16[11,128,1024]{2,1,0:T(8,128)(2,1)}, bf16[11,128,1024]{2,1,0:T(8,128)(2,1)}, u32[]{:S(2)}, u32[]{:S(2)}) %collective-permute-start.1) | collective-permute-done | bytes 2883616 | tf_op jit(solution)/shard_map/ppermute | solution.py:14
  110.5 6.8 %pad_maximum_fusion = bf16[35,128,1024]{2,1,0:T(8,128)(2,1)} fusion(bf16[11,128,1024]{2,1,0:T(8,128)(2,1)} %collective-permute-done.1, bf16[12,128,1024]{2,1,0:T(8,128)(2,1)} %collective-permute-done, bf16[12,128,1024]{2,1,0:T(8,128)(2,1)S(1)} %bitcast.61), kind=kLoop, calls=%fused_computation.7 | loop fusion | flops 9175040 | bytes 18350080 | tf_op jit(solution)/shard_map/concatenate | solution.py:34
  117.3 74.0 %while.18 = (s32[]{:T(128)}, f32[12,128]{1,0:T(8,128)S(1)}, f32[35,128]{1,0:T(8,128)S(1)}, pred[12,23]{0,1:T(8,128)(4,1)S(1)}, bf16[35,128,1024]{2,1,0:T(8,128)(...) while((s32[]{:T(128)}, f32[12,128]{1,0:T(8,128)S(1)}, ...), condition=%wide.region_6.7_spmd.clone, body=%wide.region_3.6_spmd.clone.sunk | while | flops 403244544 | bytes 6353093 | solution.py:69
  117.3 3.0 %fusion.18 = (f32[12,128]{1,0:T(8,128)S(1)}, f32[12,128]{1,0:T(8,128)S(1)}) fusion(bf16[12,128,1024]{2,1,0:T(8,128)(2,1)S(1)} %get-tuple-element.303, bf16[35,128,1024]{2,1,0:T(8,128)(2,1)} %get-tuple-element.302, s32[]{:T(128)S(6)} %select_n.60, pred[12]{0:T(512)(128)(4,1)S(1)} %dynamic-slice_bitcast_fusion.2), kind=kOutput, calls=%fused_computation.45.clone.1 | convolution fusion | flops 403239936 | bytes 6303760 | tf_op jit(solution)/shard_map/while/body/eval_jaxpr/hic,hjc->hij/dot_general | solution.py:55
  120.3 0.2 dynamic_update_slice.16
  120.6 3.0 %fusion.18 = (f32[12,128]{1,0:T(8,128)S(1)}, f32[12,128]{1,0:T(8,128)S(1)}) fusion(bf16[12,128,1024]{2,1,0:T(8,128)(2,1)S(1)} %get-tuple-element.303, bf16[35,128,1024]{2,1,0:T(8,128)(2,1)} %get-tuple-element.302, s32[]{:T(128)S(6)} %select_n.60, pred[12]{0:T(512)(128)(4,1)S(1)} %dynamic-slice_bitcast_fusion.2), kind=kOutput, calls=%fused_computation.45.clone.1 | convolution fusion | flops 403239936 | bytes 6303760 | tf_op jit(solution)/shard_map/while/body/eval_jaxpr/hic,hjc->hij/dot_general | solution.py:55
  123.5 0.2 dynamic_update_slice.16
  123.8 3.0 %fusion.18 = (f32[12,128]{1,0:T(8,128)S(1)}, f32[12,128]{1,0:T(8,128)S(1)}) fusion(bf16[12,128,1024]{2,1,0:T(8,128)(2,1)S(1)} %get-tuple-element.303, bf16[35,128,1024]{2,1,0:T(8,128)(2,1)} %get-tuple-element.302, s32[]{:T(128)S(6)} %select_n.60, pred[12]{0:T(512)(128)(4,1)S(1)} %dynamic-slice_bitcast_fusion.2), kind=kOutput, calls=%fused_computation.45.clone.1 | convolution fusion | flops 403239936 | bytes 6303760 | tf_op jit(solution)/shard_map/while/body/eval_jaxpr/hic,hjc->hij/dot_general | solution.py:55
  126.8 0.2 dynamic_update_slice.16
  127.0 3.0 %fusion.18 = (f32[12,128]{1,0:T(8,128)S(1)}, f32[12,128]{1,0:T(8,128)S(1)}) fusion(bf16[12,128,1024]{2,1,0:T(8,128)(2,1)S(1)} %get-tuple-element.303, bf16[35,128,1024]{2,1,0:T(8,128)(2,1)} %get-tuple-element.302, s32[]{:T(128)S(6)} %select_n.60, pred[12]{0:T(512)(128)(4,1)S(1)} %dynamic-slice_bitcast_fusion.2), kind=kOutput, calls=%fused_computation.45.clone.1 | convolution fusion | flops 403239936 | bytes 6303760 | tf_op jit(solution)/shard_map/while/body/eval_jaxpr/hic,hjc->hij/dot_general | solution.py:55
  130.0 0.2 dynamic_update_slice.16
  130.2 3.0 %fusion.18 = (f32[12,128]{1,0:T(8,128)S(1)}, f32[12,128]{1,0:T(8,128)S(1)}) fusion(bf16[12,128,1024]{2,1,0:T(8,128)(2,1)S(1)} %get-tuple-element.303, bf16[35,128,1024]{2,1,0:T(8,128)(2,1)} %get-tuple-element.302, s32[]{:T(128)S(6)} %select_n.60, pred[12]{0:T(512)(128)(4,1)S(1)} %dynamic-slice_bitcast_fusion.2), kind=kOutput, calls=%fused_computation.45.clone.1 | convolution fusion | flops 403239936 | bytes 6303760 | tf_op jit(solution)/shard_map/while/body/eval_jaxpr/hic,hjc->hij/dot_general | solution.py:55
  133.2 0.2 dynamic_update_slice.16
  133.5 3.0 %fusion.18 = (f32[12,128]{1,0:T(8,128)S(1)}, f32[12,128]{1,0:T(8,128)S(1)}) fusion(bf16[12,128,1024]{2,1,0:T(8,128)(2,1)S(1)} %get-tuple-element.303, bf16[35,128,1024]{2,1,0:T(8,128)(2,1)} %get-tuple-element.302, s32[]{:T(128)S(6)} %select_n.60, pred[12]{0:T(512)(128)(4,1)S(1)} %dynamic-slice_bitcast_fusion.2), kind=kOutput, calls=%fused_computation.45.clone.1 | convolution fusion | flops 403239936 | bytes 6303760 | tf_op jit(solution)/shard_map/while/body/eval_jaxpr/hic,hjc->hij/dot_general | solution.py:55
  136.4 0.2 dynamic_update_slice.16
  136.7 3.0 %fusion.18 = (f32[12,128]{1,0:T(8,128)S(1)}, f32[12,128]{1,0:T(8,128)S(1)}) fusion(bf16[12,128,1024]{2,1,0:T(8,128)(2,1)S(1)} %get-tuple-element.303, bf16[35,128,1024]{2,1,0:T(8,128)(2,1)} %get-tuple-element.302, s32[]{:T(128)S(6)} %select_n.60, pred[12]{0:T(512)(128)(4,1)S(1)} %dynamic-slice_bitcast_fusion.2), kind=kOutput, calls=%fused_computation.45.clone.1 | convolution fusion | flops 403239936 | bytes 6303760 | tf_op jit(solution)/shard_map/while/body/eval_jaxpr/hic,hjc->hij/dot_general | solution.py:55
  139.7 0.2 dynamic_update_slice.16
  139.9 3.0 %fusion.18 = (f32[12,128]{1,0:T(8,128)S(1)}, f32[12,128]{1,0:T(8,128)S(1)}) fusion(bf16[12,128,1024]{2,1,0:T(8,128)(2,1)S(1)} %get-tuple-element.303, bf16[35,128,1024]{2,1,0:T(8,128)(2,1)} %get-tuple-element.302, s32[]{:T(128)S(6)} %select_n.60, pred[12]{0:T(512)(128)(4,1)S(1)} %dynamic-slice_bitcast_fusion.2), kind=kOutput, calls=%fused_computation.45.clone.1 | convolution fusion | flops 403239936 | bytes 6303760 | tf_op jit(solution)/shard_map/while/body/eval_jaxpr/hic,hjc->hij/dot_general | solution.py:55
  142.9 0.2 dynamic_update_slice.16
  143.1 3.0 %fusion.18 = (f32[12,128]{1,0:T(8,128)S(1)}, f32[12,128]{1,0:T(8,128)S(1)}) fusion(bf16[12,128,1024]{2,1,0:T(8,128)(2,1)S(1)} %get-tuple-element.303, bf16[35,128,1024]{2,1,0:T(8,128)(2,1)} %get-tuple-element.302, s32[]{:T(128)S(6)} %select_n.60, pred[12]{0:T(512)(128)(4,1)S(1)} %dynamic-slice_bitcast_fusion.2), kind=kOutput, calls=%fused_computation.45.clone.1 | convolution fusion | flops 403239936 | bytes 6303760 | tf_op jit(solution)/shard_map/while/body/eval_jaxpr/hic,hjc->hij/dot_general | solution.py:55
  146.1 0.2 dynamic_update_slice.16
  146.4 3.0 %fusion.18 = (f32[12,128]{1,0:T(8,128)S(1)}, f32[12,128]{1,0:T(8,128)S(1)}) fusion(bf16[12,128,1024]{2,1,0:T(8,128)(2,1)S(1)} %get-tuple-element.303, bf16[35,128,1024]{2,1,0:T(8,128)(2,1)} %get-tuple-element.302, s32[]{:T(128)S(6)} %select_n.60, pred[12]{0:T(512)(128)(4,1)S(1)} %dynamic-slice_bitcast_fusion.2), kind=kOutput, calls=%fused_computation.45.clone.1 | convolution fusion | flops 403239936 | bytes 6303760 | tf_op jit(solution)/shard_map/while/body/eval_jaxpr/hic,hjc->hij/dot_general | solution.py:55
  149.3 0.2 dynamic_update_slice.16
  149.6 3.0 %fusion.18 = (f32[12,128]{1,0:T(8,128)S(1)}, f32[12,128]{1,0:T(8,128)S(1)}) fusion(bf16[12,128,1024]{2,1,0:T(8,128)(2,1)S(1)} %get-tuple-element.303, bf16[35,128,1024]{2,1,0:T(8,128)(2,1)} %get-tuple-element.302, s32[]{:T(128)S(6)} %select_n.60, pred[12]{0:T(512)(128)(4,1)S(1)} %dynamic-slice_bitcast_fusion.2), kind=kOutput, calls=%fused_computation.45.clone.1 | convolution fusion | flops 403239936 | bytes 6303760 | tf_op jit(solution)/shard_map/while/body/eval_jaxpr/hic,hjc->hij/dot_general | solution.py:55
  152.6 0.2 dynamic_update_slice.16
  152.8 3.0 %fusion.18 = (f32[12,128]{1,0:T(8,128)S(1)}, f32[12,128]{1,0:T(8,128)S(1)}) fusion(bf16[12,128,1024]{2,1,0:T(8,128)(2,1)S(1)} %get-tuple-element.303, bf16[35,128,1024]{2,1,0:T(8,128)(2,1)} %get-tuple-element.302, s32[]{:T(128)S(6)} %select_n.60, pred[12]{0:T(512)(128)(4,1)S(1)} %dynamic-slice_bitcast_fusion.2), kind=kOutput, calls=%fused_computation.45.clone.1 | convolution fusion | flops 403239936 | bytes 6303760 | tf_op jit(solution)/shard_map/while/body/eval_jaxpr/hic,hjc->hij/dot_general | solution.py:55
  155.8 0.2 dynamic_update_slice.16
  156.0 3.0 %fusion.18 = (f32[12,128]{1,0:T(8,128)S(1)}, f32[12,128]{1,0:T(8,128)S(1)}) fusion(bf16[12,128,1024]{2,1,0:T(8,128)(2,1)S(1)} %get-tuple-element.303, bf16[35,128,1024]{2,1,0:T(8,128)(2,1)} %get-tuple-element.302, s32[]{:T(128)S(6)} %select_n.60, pred[12]{0:T(512)(128)(4,1)S(1)} %dynamic-slice_bitcast_fusion.2), kind=kOutput, calls=%fused_computation.45.clone.1 | convolution fusion | flops 403239936 | bytes 6303760 | tf_op jit(solution)/shard_map/while/body/eval_jaxpr/hic,hjc->hij/dot_general | solution.py:55
  159.0 0.2 dynamic_update_slice.16
  159.3 3.0 %fusion.18 = (f32[12,128]{1,0:T(8,128)S(1)}, f32[12,128]{1,0:T(8,128)S(1)}) fusion(bf16[12,128,1024]{2,1,0:T(8,128)(2,1)S(1)} %get-tuple-element.303, bf16[35,128,1024]{2,1,0:T(8,128)(2,1)} %get-tuple-element.302, s32[]{:T(128)S(6)} %select_n.60, pred[12]{0:T(512)(128)(4,1)S(1)} %dynamic-slice_bitcast_fusion.2), kind=kOutput, calls=%fused_computation.45.clone.1 | convolution fusion | flops 403239936 | bytes 6303760 | tf_op jit(solution)/shard_map/while/body/eval_jaxpr/hic,hjc->hij/dot_general | solution.py:55
  162.3 0.2 dynamic_update_slice.16
  162.5 3.0 %fusion.18 = (f32[12,128]{1,0:T(8,128)S(1)}, f32[12,128]{1,0:T(8,128)S(1)}) fusion(bf16[12,128,1024]{2,1,0:T(8,128)(2,1)S(1)} %get-tuple-element.303, bf16[35,128,1024]{2,1,0:T(8,128)(2,1)} %get-tuple-element.302, s32[]{:T(128)S(6)} %select_n.60, pred[12]{0:T(512)(128)(4,1)S(1)} %dynamic-slice_bitcast_fusion.2), kind=kOutput, calls=%fused_computation.45.clone.1 | convolution fusion | flops 403239936 | bytes 6303760 | tf_op jit(solution)/shard_map/while/body/eval_jaxpr/hic,hjc->hij/dot_general | solution.py:55
  165.5 0.2 dynamic_update_slice.16
  165.7 3.0 %fusion.18 = (f32[12,128]{1,0:T(8,128)S(1)}, f32[12,128]{1,0:T(8,128)S(1)}) fusion(bf16[12,128,1024]{2,1,0:T(8,128)(2,1)S(1)} %get-tuple-element.303, bf16[35,128,1024]{2,1,0:T(8,128)(2,1)} %get-tuple-element.302, s32[]{:T(128)S(6)} %select_n.60, pred[12]{0:T(512)(128)(4,1)S(1)} %dynamic-slice_bitcast_fusion.2), kind=kOutput, calls=%fused_computation.45.clone.1 | convolution fusion | flops 403239936 | bytes 6303760 | tf_op jit(solution)/shard_map/while/body/eval_jaxpr/hic,hjc->hij/dot_general | solution.py:55
  168.7 0.2 dynamic_update_slice.16
  168.9 3.0 %fusion.18 = (f32[12,128]{1,0:T(8,128)S(1)}, f32[12,128]{1,0:T(8,128)S(1)}) fusion(bf16[12,128,1024]{2,1,0:T(8,128)(2,1)S(1)} %get-tuple-element.303, bf16[35,128,1024]{2,1,0:T(8,128)(2,1)} %get-tuple-element.302, s32[]{:T(128)S(6)} %select_n.60, pred[12]{0:T(512)(128)(4,1)S(1)} %dynamic-slice_bitcast_fusion.2), kind=kOutput, calls=%fused_computation.45.clone.1 | convolution fusion | flops 403239936 | bytes 6303760 | tf_op jit(solution)/shard_map/while/body/eval_jaxpr/hic,hjc->hij/dot_general | solution.py:55
  171.9 0.2 dynamic_update_slice.16
  172.1 3.0 %fusion.18 = (f32[12,128]{1,0:T(8,128)S(1)}, f32[12,128]{1,0:T(8,128)S(1)}) fusion(bf16[12,128,1024]{2,1,0:T(8,128)(2,1)S(1)} %get-tuple-element.303, bf16[35,128,1024]{2,1,0:T(8,128)(2,1)} %get-tuple-element.302, s32[]{:T(128)S(6)} %select_n.60, pred[12]{0:T(512)(128)(4,1)S(1)} %dynamic-slice_bitcast_fusion.2), kind=kOutput, calls=%fused_computation.45.clone.1 | convolution fusion | flops 403239936 | bytes 6303760 | tf_op jit(solution)/shard_map/while/body/eval_jaxpr/hic,hjc->hij/dot_general | solution.py:55
  175.1 0.2 dynamic_update_slice.16
  175.4 3.0 %fusion.18 = (f32[12,128]{1,0:T(8,128)S(1)}, f32[12,128]{1,0:T(8,128)S(1)}) fusion(bf16[12,128,1024]{2,1,0:T(8,128)(2,1)S(1)} %get-tuple-element.303, bf16[35,128,1024]{2,1,0:T(8,128)(2,1)} %get-tuple-element.302, s32[]{:T(128)S(6)} %select_n.60, pred[12]{0:T(512)(128)(4,1)S(1)} %dynamic-slice_bitcast_fusion.2), kind=kOutput, calls=%fused_computation.45.clone.1 | convolution fusion | flops 403239936 | bytes 6303760 | tf_op jit(solution)/shard_map/while/body/eval_jaxpr/hic,hjc->hij/dot_general | solution.py:55
  178.3 0.2 dynamic_update_slice.16
  178.6 3.0 %fusion.18 = (f32[12,128]{1,0:T(8,128)S(1)}, f32[12,128]{1,0:T(8,128)S(1)}) fusion(bf16[12,128,1024]{2,1,0:T(8,128)(2,1)S(1)} %get-tuple-element.303, bf16[35,128,1024]{2,1,0:T(8,128)(2,1)} %get-tuple-element.302, s32[]{:T(128)S(6)} %select_n.60, pred[12]{0:T(512)(128)(4,1)S(1)} %dynamic-slice_bitcast_fusion.2), kind=kOutput, calls=%fused_computation.45.clone.1 | convolution fusion | flops 403239936 | bytes 6303760 | tf_op jit(solution)/shard_map/while/body/eval_jaxpr/hic,hjc->hij/dot_general | solution.py:55
  181.5 0.2 dynamic_update_slice.16
  181.8 3.0 %fusion.18 = (f32[12,128]{1,0:T(8,128)S(1)}, f32[12,128]{1,0:T(8,128)S(1)}) fusion(bf16[12,128,1024]{2,1,0:T(8,128)(2,1)S(1)} %get-tuple-element.303, bf16[35,128,1024]{2,1,0:T(8,128)(2,1)} %get-tuple-element.302, s32[]{:T(128)S(6)} %select_n.60, pred[12]{0:T(512)(128)(4,1)S(1)} %dynamic-slice_bitcast_fusion.2), kind=kOutput, calls=%fused_computation.45.clone.1 | convolution fusion | flops 403239936 | bytes 6303760 | tf_op jit(solution)/shard_map/while/body/eval_jaxpr/hic,hjc->hij/dot_general | solution.py:55
  184.8 0.2 dynamic_update_slice.16
  185.0 3.0 %fusion.18 = (f32[12,128]{1,0:T(8,128)S(1)}, f32[12,128]{1,0:T(8,128)S(1)}) fusion(bf16[12,128,1024]{2,1,0:T(8,128)(2,1)S(1)} %get-tuple-element.303, bf16[35,128,1024]{2,1,0:T(8,128)(2,1)} %get-tuple-element.302, s32[]{:T(128)S(6)} %select_n.60, pred[12]{0:T(512)(128)(4,1)S(1)} %dynamic-slice_bitcast_fusion.2), kind=kOutput, calls=%fused_computation.45.clone.1 | convolution fusion | flops 403239936 | bytes 6303760 | tf_op jit(solution)/shard_map/while/body/eval_jaxpr/hic,hjc->hij/dot_general | solution.py:55
  188.0 0.2 dynamic_update_slice.16
  188.2 3.0 %fusion.18 = (f32[12,128]{1,0:T(8,128)S(1)}, f32[12,128]{1,0:T(8,128)S(1)}) fusion(bf16[12,128,1024]{2,1,0:T(8,128)(2,1)S(1)} %get-tuple-element.303, bf16[35,128,1024]{2,1,0:T(8,128)(2,1)} %get-tuple-element.302, s32[]{:T(128)S(6)} %select_n.60, pred[12]{0:T(512)(128)(4,1)S(1)} %dynamic-slice_bitcast_fusion.2), kind=kOutput, calls=%fused_computation.45.clone.1 | convolution fusion | flops 403239936 | bytes 6303760 | tf_op jit(solution)/shard_map/while/body/eval_jaxpr/hic,hjc->hij/dot_general | solution.py:55
  191.2 0.2 dynamic_update_slice.16
  191.4 0.3 dynamic_update_slice.13
  191.7 0.6 copy-done.1
  192.4 1.0 fusion.8
  193.4 88.6 %all-reduce.3.cloned.1.call-done = f32[215,128]{1,0:T(8,128)} async-done(((f32[215,128]{1,0:T(8,128)}), f32[215,128]{1,0:T(8,128)}) %all-reduce.3.cloned.1.call-update) | async-done | bytes 110096 | tf_op jit(solution)/shard_map/pmax | solution.py:81
  282.0 1.3 maximum_bitcast_fusion
  (89 shorter events, 3.3 us)
Async XLA Ops:
  6.5 275.4 %all-reduce.3.cloned.1.call-start = ((), (), s32[]{:S(2)}) async-start(), calls=%async_computation | async-start | bytes 221184 | tf_op jit(solution)/shard_map/pmax | solution.py:81
  6.5 2.8 copy-start
  10.0 7.1 %copy-start.3 = (s32[192]{0:T(256)S(1)}, s32[192]{0:T(256)}, u32[]{:S(2)}) copy-start(s32[192]{0:T(256)} %param.6) | copy-start | bytes 2308
  10.0 9.6 %copy-start.2 = (s32[210,2]{0,1:T(2,128)S(1)}, s32[210,2]{0,1:T(2,128)}, u32[]{:S(2)}) copy-start(s32[210,2]{0,1:T(2,128)} %param.7) | copy-start | bytes 5044
  10.0 100.6 %collective-permute-start = (bf16[12,128,1024]{2,1,0:T(8,128)(2,1)S(1)}, bf16[12,128,1024]{2,1,0:T(8,128)(2,1)}, u32[]{:S(2)}, u32[]{:S(2)}) collective-permute-start(bf16[12,128,1024]{2,1,0:T(8,128)(2,1)S(1)} %bitcast.60), channel_id=1, source_target_pairs={{1,0},{2,1},{3,2},{4,3},{5,4},{6,5},{7,6},{8,7},{9,8},{10,9},{11,1... | collective-permute-start | bytes 9437192 | tf_op jit(solution)/shard_map/ppermute | solution.py:14
  14.6 96.0 %collective-permute-start.1 = (bf16[11,128,1024]{2,1,0:T(8,128)(2,1)}, bf16[11,128,1024]{2,1,0:T(8,128)(2,1)}, u32[]{:S(2)}, u32[]{:S(2)}) collective-permute-start(bf16[11,128,1024]{2,1,0:T(8,128)(2,1)} %bitcast.25), channel_id=1, source_target_pairs={{2,0},{3,1},{4,2},{5,3},{6,4},{7,5},{8,6},{9,7},{10,8},{11,9},{12,... | collective-permute-start | bytes 8650760 | tf_op jit(solution)/shard_map/ppermute | solution.py:14
  191.7 0.6 copy-start.1
Sparse Core Ops, SparseCore 0:
  192.5 89.3 all-reduce.2
where the time goes:
time: 291 us; the launch traced here: 290 us
  waiting for transfers between devices  179 us (62%)
  matrix products  68.9 us (24%)
  between operations  13.6 us (5%)
  other arithmetic  12 us (4%)
  local copies, waits for them, and re-layouts  10.2 us (4%)
  starting transfers between devices  5.23 us (2%)
    ppermute x2, waiting for transfers between devices, shifted(): return lax.ppermute(block, axis, route)  90.4 us
    pmax x1, waiting for transfers between devices, on_device(): combined = lax.pmax(everything, 'rows')  88.6 us
    dot_general x23, matrix products, band_step(): jnp.einsum('hic,hjc->hij', resident_blocks, companion_row, preferred_elem...  67.9 us
    concatenate x1, other arithmetic, on_device(): block_pool = jnp.concatenate(pieces, axis=0)  6.77 us
  transfers between devices with their start and end apart: 3, of which 2 were waited for; matrix products, arithmetic and copies ran while one was open for 2% of the time, Pallas kernels for 0%

commit v1 on v0

v1 whole, which is shorter than its diff:
```python
import functools

import jax
import jax.numpy as jnp
from jax import lax
from jax.experimental import pallas as pl
from jax.experimental.pallas import tpu as pltpu
from jax.sharding import PartitionSpec as P

BLOCK = 128
NEVER = -3.0
MIB = 1 << 20
FAR_AWAY = 1 << 20
SMEM = pltpu.SMEM
VMEM = pltpu.VMEM


def plan_kernel(chip_blocks, cluster_ref, plan_ref, left_part, right_part, from_left, turn):
    here = chip_blocks // 2
    chips = cluster_ref.shape[0] // chip_blocks
    me = lax.axis_index("rows")

    def run_length(start, step):
        count = jnp.int32(0)
        for jump in (16, 8, 4, 2, 1):
            further = count + jump
            same = cluster_ref[start + step * further] == cluster_ref[start]
            count = jnp.where(same, further, count)
        return count

    def cost(blocks):
        return jnp.where(blocks > here, FAR_AWAY, blocks)

    def forward(boundary, carry):
        best_left, best_right, load_right = carry
        edge = (boundary + 1) * chip_blocks
        behind = run_length(edge, -1)
        ahead = run_length(edge - 1, 1)
        left_part[boundary] = behind
        right_part[boundary] = ahead
        by_left = jnp.maximum(best_left, cost(ahead))
        by_right = jnp.maximum(best_right, load_right + cost(ahead))
        from_left[boundary] = jnp.where(by_left <= by_right, 0, 1)
        stays_right = jnp.maximum(best_right, load_right)
        from_left[chips + boundary] = jnp.where(best_left <= stays_right, 0, 1)
        return jnp.minimum(by_left, by_right), jnp.minimum(best_left, stays_right), cost(behind)

    best_left, best_right, load_right = lax.fori_loop(
        0, chips - 1, forward, (jnp.int32(0), jnp.int32(FAR_AWAY), jnp.int32(0))
    )
    last = jnp.where(best_left <= jnp.maximum(best_right, load_right), 0, 1)

    def backward(step, state):
        boundary = chips - 2 - step
        turn[boundary] = state
        return from_left[state * chips + boundary]

    lax.fori_loop(0, chips - 1, backward, last)
    upper = lax.rem(me, 2)
    mine = lax.div(me, 2) - 1 + upper
    inside = (mine >= 0) & (mine < chips - 1)
    mine = jnp.clip(mine, 0, chips - 2)
    behind, ahead, rightwards = left_part[mine], right_part[mine], turn[mine]
    live = inside & (behind > 0) & (ahead > 0)
    receives = live & (rightwards != upper)
    sent = jnp.where(rightwards == 1, behind, ahead)
    paired = jnp.where(rightwards == 1, ahead, behind)
    plan_ref[0] = jnp.where(live, 1 + rightwards, 0)
    plan_ref[1] = jnp.where(receives, sent, 0)
    plan_ref[2] = jnp.where(receives, jnp.minimum(paired, here), 0)
    plan_ref[3] = jnp.where(receives, jnp.maximum(paired - here, 0), 0)
    plan_ref[4] = upper
    plan_ref[5] = me * here
    plan_ref[6] = (me + 1 - 2 * upper) * here
    plan_ref[7] = jnp.where(live & (rightwards == upper), sent, 0)


def make_plan(block_cluster, chip_blocks):
    chips = block_cluster.shape[0] // chip_blocks
    return pl.pallas_call(
        functools.partial(plan_kernel, chip_blocks),
        out_shape=jax.ShapeDtypeStruct((8,), jnp.int32),
        in_specs=[pl.BlockSpec(memory_space=SMEM)],
        out_specs=pl.BlockSpec(memory_space=SMEM),
        scratch_shapes=[
            SMEM((chips,), jnp.int32),
            SMEM((chips,), jnp.int32),
            SMEM((2 * chips,), jnp.int32),
            SMEM((chips,), jnp.int32),
        ],
    )(block_cluster)


def unit(rows):
    broadened = rows.astype(jnp.float32)
    total = jnp.sum(broadened * broadened, axis=1, keepdims=True)
    return (broadened * lax.rsqrt(total + 1e-06)).astype(jnp.bfloat16)


def products(left, right):
    return lax.dot_general(
        left, right, (((1,), (1,)), ((), ())), preferred_element_type=jnp.float32
    )


def local_kernel(same_device, cluster_ref, plan_ref, rows_ref, own_ref, best_ref):
    blocks = own_ref.shape[0] // BLOCK
    own_first = plan_ref[5]
    rows_first = plan_ref[5] if same_device else plan_ref[6]
    tall, wide = 4, 2

    def tile(turn, _):
        best = [jnp.full((1, BLOCK), NEVER, jnp.float32) for _ in range(wide)]
        own_rows = own_ref[pl.ds(pl.multiple_of(turn * wide * BLOCK, wide * BLOCK), wide * BLOCK), :]
        for part in range(blocks // tall):
            product = products(rows_ref[part * tall * BLOCK : (part + 1) * tall * BLOCK, :], own_rows)
            if same_device:
                row = lax.broadcasted_iota(jnp.int32, product.shape, 0) + part * tall * BLOCK
                column = lax.broadcasted_iota(jnp.int32, product.shape, 1) + turn * wide * BLOCK
                product = jnp.where(row == column, NEVER, product)
            for i in range(tall):
                for j in range(wide):
                    same = (
                        cluster_ref[rows_first + part * tall + i]
                        == cluster_ref[own_first + turn * wide + j]
                    )
                    piece = product[i * BLOCK : (i + 1) * BLOCK, j * BLOCK : (j + 1) * BLOCK]
                    top = jnp.max(piece, axis=0, keepdims=True)
                    best[j] = jnp.maximum(best[j], jnp.where(same, top, NEVER))
        for j in range(wide):
            best_ref[pl.ds(turn * wide + j, 1), :] = best[j]
        return 0

    lax.fori_loop(0, blocks // wide, tile, 0)


def local_best(same_device, block_cluster, plan, rows, own):
    blocks = own.shape[0] // BLOCK
    flops = 2 * rows.shape[0] * own.shape[0] * own.shape[1]
    return pl.pallas_call(
        functools.partial(local_kernel, same_device),
        out_shape=jax.ShapeDtypeStruct((blocks, BLOCK), jnp.float32),
        in_specs=[pl.BlockSpec(memory_space=SMEM)] * 2 + [pl.BlockSpec(memory_space=VMEM)] * 2,
        out_specs=pl.BlockSpec(memory_space=VMEM),
        compiler_params=pltpu.CompilerParams(vmem_limit_bytes=24 * MIB),
        cost_estimate=pl.CostEstimate(flops=flops, bytes_accessed=4 * rows.size, transcendentals=0),
    )(block_cluster, plan, rows, own)


def cross_kernel(plan_ref, got_ref, own_ref, other_ref, back_ref, own_best_ref, other_best_ref, rows, row_best):
    blocks = got_ref.shape[0] // BLOCK
    count, near, far, upper = plan_ref[1], plan_ref[2], plan_ref[3], plan_ref[4]
    tall, wide = 4, 2
    back_ref[...] = jnp.full(back_ref.shape, NEVER, jnp.float32)
    own_best_ref[...] = jnp.full(own_best_ref.shape, NEVER, jnp.float32)
    other_best_ref[...] = jnp.full(other_best_ref.shape, NEVER, jnp.float32)
    got_from = jnp.where(upper == 1, 0, blocks - count)
    got_to = got_from + count

    def against(side_ref, best_ref, part, lowest, highest):
        def tile(turn, _):
            side = side_ref[pl.ds(pl.multiple_of(turn * wide * BLOCK, wide * BLOCK), wide * BLOCK), :]
            product = products(rows[...], side)
            best = [jnp.full((1, BLOCK), NEVER, jnp.float32) for _ in range(wide)]
            for j in range(wide):
                block = turn * wide + j
                fits = (block >= lowest) & (block < highest)
                for i in range(tall):
                    piece = product[i * BLOCK : (i + 1) * BLOCK, j * BLOCK : (j + 1) * BLOCK]
                    held = row_best[i * BLOCK : (i + 1) * BLOCK, :]
                    row_best[i * BLOCK : (i + 1) * BLOCK, :] = jnp.maximum(
                        held, jnp.where(fits, piece, NEVER)
                    )
                    valid = (part * tall + i >= got_from) & (part * tall + i < got_to) & fits
                    top = jnp.max(piece, axis=0, keepdims=True)
                    best[j] = jnp.maximum(best[j], jnp.where(valid, top, NEVER))
                at = pl.ds(block, 1)
                best_ref[at, :] = jnp.maximum(best_ref[at, :], best[j])
            return 0

        lax.fori_loop(lax.div(lowest, wide), lax.div(highest + wide - 1, wide), tile, 0)

    def chunk(part, _):
        start = pl.multiple_of(part * tall * BLOCK, tall * BLOCK)
        rows[...] = unit(got_ref[pl.ds(start, tall * BLOCK), :])
        row_best[...] = jnp.full(row_best.shape, NEVER, jnp.float32)
        near_from = jnp.where(upper == 1, blocks - near, 0)
        against(own_ref, own_best_ref, part, near_from, near_from + near)
        far_from = jnp.where(upper == 1, blocks - far, 0)
        against(other_ref, other_best_ref, part, far_from, far_from + far)
        for i in range(tall):
            block = part * tall + i
            valid = (block >= got_from) & (block < got_to)
            top = jnp.max(row_best[i * BLOCK : (i + 1) * BLOCK, :].T, axis=0, keepdims=True)
            back_ref[pl.ds(block, 1), :] = jnp.where(valid, top, NEVER)
        return 0

    lax.fori_loop(lax.div(got_from, tall), lax.div(got_to + tall - 1, tall), chunk, 0)


def cross_best(plan, got, own, other):
    blocks = own.shape[0] // BLOCK
    features = own.shape[1]
    out = jax.ShapeDtypeStruct((blocks, BLOCK), jnp.float32)
    vmem = pl.BlockSpec(memory_space=VMEM)
    return pl.pallas_call(
        cross_kernel,
        out_shape=(out, out, out),
        in_specs=[pl.BlockSpec(memory_space=SMEM)] + [vmem] * 3,
        out_specs=(vmem, vmem, vmem),
        scratch_shapes=[VMEM((4 * BLOCK, features), jnp.bfloat16), VMEM((4 * BLOCK, BLOCK), jnp.float32)],
        compiler_params=pltpu.CompilerParams(vmem_limit_bytes=24 * MIB),
        cost_estimate=pl.CostEstimate(
            flops=2 * own.shape[0] * own.shape[0] * features, bytes_accessed=6 * own.size, transcendentals=0
        ),
    )(plan, got, own, other)


def on_device(embeddings, block_cluster, pair_blocks):
    blocks = embeddings.shape[0] // BLOCK
    devices = lax.axis_size("rows")
    swap = [(i, i ^ 1) for i in range(devices)]
    leftwards = [(i + 1, i) for i in range(1, devices - 1, 2)]
    rightwards = [(b, a) for a, b in leftwards]

    plan = make_plan(block_cluster, 2 * blocks)
    own = unit(embeddings)
    other = lax.ppermute(own, "rows", swap)

    def send(route):
        def branch(embeddings, own):
            got = lax.ppermute(embeddings, "rows", route)
            return got, local_best(True, block_cluster, plan, own, own)

        return branch

    def stay(embeddings, own):
        return embeddings, local_best(True, block_cluster, plan, own, own)

    got, best = lax.switch(plan[0], [stay, send(leftwards), send(rightwards)], embeddings, own)
    back, own_best, other_best = cross_best(plan, got, own, other)

    def answer(route):
        def branch(back, own, other):
            returned = lax.ppermute(back, "rows", route)
            return returned, local_best(False, block_cluster, plan, other, own)

        return branch

    def silent(back, own, other):
        return back, local_best(False, block_cluster, plan, other, own)

    returned, beside = lax.switch(
        plan[0], [silent, answer(rightwards), answer(leftwards)], back, own, other
    )
    from_core = lax.ppermute(other_best, "rows", swap)
    best = jnp.maximum(jnp.maximum(best, beside), jnp.maximum(own_best, from_core))
    best = jnp.where(plan[7] > 0, jnp.maximum(best, returned), best)
    return best.reshape(-1)


def solution(mesh):
    placed = (P(("groups", "rows"), None), P("groups"), P(("groups", "rows"), None))
    return jax.shard_map(
        on_device, mesh=mesh, in_specs=placed, out_specs=P(("groups", "rows")), check_vma=False
    )
```

time: 291 us -> 77.6 us (0.27)
  the two profiles are of different devices: /device:TPU:8 before, /device:TPU:1 now
where the time goes in v1:
time: 77.6 us; the launch traced here: 77.5 us
  Pallas kernels  34.2 us (44%)
  waiting for transfers between devices  28.4 us (37%)
  starting transfers between devices  7.09 us (9%)
  other arithmetic  3.51 us (5%)
  local copies, waits for them, and re-layouts  2.79 us (4%)
  between operations  1.36 us (2%)
    ppermute x1, waiting for transfers between devices, branch(): got = lax.ppermute(embeddings, 'rows', route)  28.4 us
    pallas_call x2, Pallas kernels, local_best(): pl.pallas_call(functools.partial(local_kernel, same_device), out_shape=ja...  18.1 us
    pallas_call x1, Pallas kernels, cross_best(): pl.pallas_call(cross_kernel, out_shape=(out, out, out), in_specs=[pl.Bloc...  14.6 us
    ppermute x1, starting transfers between devices, branch(): returned = lax.ppermute(back, 'rows', route)  5.67 us
    convert_element_type x1, other arithmetic, unit(): return (broadened * lax.rsqrt(total + 1e-06)).astype(jnp.bfloat16)  2.21 us
    unnamed x3, local copies, waits for them, and re-layouts  1.9 us
  transfers between devices with their start and end apart: 4, of which 1 were waited for; matrix products, arithmetic and copies ran while one was open for 1% of the time, Pallas kernels for 25%

profile of v1, /device:TPU:1, one launch (start us, length us, event | category | flops | bytes accessed | tf_op | source)
XLA Modules:
  0.0 77.5 jit_solution(11936966870359411517)
XLA Ops:
  0.0 1.9 %copy.16 = bf16[1536,1024]{1,0:T(8,128)(2,1)S(1)} copy(bf16[1536,1024]{1,0:T(8,128)(2,1)} %param.9) | data formatting | bytes 6291456
  1.9 0.7 fusion
  2.6 0.0 copy-start
  2.6 2.2 %fusion.1.own_ref = bf16[1536,1024]{1,0:T(8,128)(2,1)} fusion(bf16[1536,1024]{1,0:T(8,128)(2,1)S(1)} %copy.16, f32[1536]{0:T(1024)S(1)} %add_rsqrt_fusion), kind=kLoop, calls=%fused_computation.3 | loop fusion | flops 4718592 | bytes 6297600 | tf_op jit(solution)/shard_map/convert_element_type | solution.py:97
  4.8 0.1 collective-permute-start.4
  4.9 0.0 copy-done
  4.9 1.5 %shard_map.28.plan_ref = s32[8]{0:T(128)S(1)} custom-call(s32[192]{0:T(256)S(1)} %copy-done), custom_call_target="tpu_custom_call" | custom-call | tf_op jit(solution)/shard_map/pallas_call | solution.py:80
  6.4 0.6 fusion.3
  7.6 39.1 %conditional.2 = (bf16[1536,1024]{1,0:T(8,128)(2,1)S(1)}, f32[12,128]{1,0:T(8,128)S(1)}) conditional(s32[]{:T(128)} %bitcast.1, (s32[192]{0:T(256)S(1)}, s32[8]{0:T(128)S(1)}, bf16[1536,1024]{1,0:T(8,128)(2,1)}, bf16[1536,1024]{1,0:T(8,128)(2,1)S(1)}) %tuple.40, (bf16[1536,1024]{1,0:T(8,128)(2,1)S(1)}, s32[192]{0:T(256)S(1)}, ...), branch_computations={%region_1.0_spmd, %region_2.0_spmd, %region_3.0_spmd} | conditional | flops 4831838208 | bytes 25165880 | solution.py:240
  7.6 1.3 %collective-permute-start = (bf16[1536,1024]{1,0:T(8,128)(2,1)S(1)}, bf16[1536,1024]{1,0:T(8,128)(2,1)S(1)}, u32[]{:S(2)}, u32[]{:S(2)}) collective-permute-start(bf16[1536,1024]{1,0:T(8,128)(2,1)S(1)} %get-tuple-element.63), channel_id=1, source_target_pairs={{2,1},{4,3},{6,5},{8,7},{10,9},{12,11},{14,13},{18,17},{20,19},{22... | collective-permute-start | bytes 9437192 | tf_op jit(solution)/shard_map/cond/branch_1_fun/ppermute | solution.py:232
  8.9 9.1 %branch_1_fun.2 = f32[12,128]{1,0:T(8,128)S(1)} custom-call(s32[192]{0:T(256)S(1)} %get-tuple-element.64.cluster_ref, s32[8]{0:T(128)S(1)} %get-tuple-element.65.plan_ref, bf16[1536,1024]{1,0:T(8,128)(2,1)} %get-tuple-element.66.rows_ref.own_ref, bf16[1536,1024]{1,0:T(8,128)(2,1)} %get-tuple-element.66.rows_ref.own_ref), custom_call_target="tpu_custom_call" | custom-call | flops 4831838208 | bytes 6291456 | tf_op jit(solution)/shard_map/cond/branch_1_fun/pallas_call | solution.py:140
  18.0 28.4 %collective-permute-done = bf16[1536,1024]{1,0:T(8,128)(2,1)S(1)} collective-permute-done((bf16[1536,1024]{1,0:T(8,128)(2,1)S(1)}, bf16[1536,1024]{1,0:T(8,128)(2,1)S(1)}, u32[]{:S(2)}, u32[]{:S(2)}) %collective-permute-start) | collective-permute-done | bytes 3145760 | tf_op jit(solution)/shard_map/cond/branch_1_fun/ppermute | solution.py:232
  46.4 0.3 copy.5
  46.7 0.0 collective-permute-done.4.other_ref
  46.8 14.6 %shard_map.29 = (f32[12,128]{1,0:T(8,128)S(1)}, f32[12,128]{1,0:T(8,128)S(1)}, f32[12,128]{1,0:T(8,128)S(1)}) custom-call(s32[8]{0:T(128)S(1)} %shard_map.28.plan_ref, bf16[1536,1024]{1,0:T(8,128)(2,1)S(1)} %get-tuple-element.94.got_ref, bf16[1536,1024]{1,0:T(8,128)(2,1)} %fusion.1.own_ref, bf16[1536,1024]{1,0:T(8,128)(2,1)} %collective-permute-done.4.other_ref), custom_call_target="tpu_custom_call" | custom-call | flops 4831838208 | bytes 9437184 | tf_op jit(solution)/shard_map/pallas_call | solution.py:206
  61.4 0.1 collective-permute-start.5
  62.1 14.8 %conditional.3 = (f32[12,128]{1,0:T(8,128)S(1)}, f32[12,128]{1,0:T(8,128)S(1)}) conditional(s32[]{:T(128)} %bitcast.1, (s32[192]{0:T(256)S(1)}, s32[8]{0:T(128)S(1)}, bf16[1536,1024]{1,0:T(8,128)(2,1)}, bf16[1536,1024]{1,0:T(8,128)(2,1)}, f32[12,128]{1,0:T(8,128)S(1)}) %tuple.43, (f32[12,128]{1,0:T(8,128)S(1)}, s32[192]{0:T(256)S(1)}, ...), branch_computations={%region_4.0_spmd, %region_5.0_spmd, %region_6.0_spmd} | conditional | flops 4831838208 | bytes 6328376 | solution.py:253
  62.1 5.7 %collective-permute-start.2 = (f32[12,128]{1,0:T(8,128)S(1)}, f32[12,128]{1,0:T(8,128)S(1)}, u32[]{:S(2)}, u32[]{:S(2)}) collective-permute-start(f32[12,128]{1,0:T(8,128)S(1)} %get-tuple-element.76), channel_id=1, source_target_pairs={{1,2},{3,4},{5,6},{7,8},{9,10},{11,12},{13,14},{17,18},{19,20},{21... | collective-permute-start | bytes 18440 | tf_op jit(solution)/shard_map/cond/branch_1_fun/ppermute | solution.py:245
  67.8 9.0 %branch_1_fun.3 = f32[12,128]{1,0:T(8,128)S(1)} custom-call(s32[192]{0:T(256)S(1)} %get-tuple-element.77.cluster_ref, s32[8]{0:T(128)S(1)} %get-tuple-element.78.plan_ref, bf16[1536,1024]{1,0:T(8,128)(2,1)} %get-tuple-element.79.rows_ref, bf16[1536,1024]{1,0:T(8,128)(2,1)} %get-tuple-element.80.own_ref), custom_call_target="tpu_custom_call" | custom-call | flops 4831838208 | bytes 6291456 | tf_op jit(solution)/shard_map/cond/branch_1_fun/pallas_call | solution.py:140
  76.8 0.0 collective-permute-done.2
  76.9 0.0 collective-permute-done.5
  76.9 0.6 fusion.2
  (2 shorter events, 0.0 us)
Async XLA Ops:
  2.6 2.3 %copy-start = (s32[192]{0:T(256)S(1)}, s32[192]{0:T(256)}, u32[]{:S(2)}) copy-start(s32[192]{0:T(256)} %cluster_ref.1) | copy-start | bytes 2308
  4.8 41.9 %collective-permute-start.4 = (bf16[1536,1024]{1,0:T(8,128)(2,1)}, bf16[1536,1024]{1,0:T(8,128)(2,1)}, u32[]{:S(2)}, u32[]{:S(2)}) collective-permute-start(bf16[1536,1024]{1,0:T(8,128)(2,1)} %fusion.1.own_ref), channel_id=1, source_target_pairs={{0,1},{1,0},{2,3},{3,2},{4,5},{5,4},{6,7},{7,6},{8,9},{9,8},{10,11... | collective-permute-start | bytes 9437192 | tf_op jit(solution)/shard_map/ppermute | solution.py:228
  7.6 38.8 %collective-permute-start = (bf16[1536,1024]{1,0:T(8,128)(2,1)S(1)}, bf16[1536,1024]{1,0:T(8,128)(2,1)S(1)}, u32[]{:S(2)}, u32[]{:S(2)}) collective-permute-start(bf16[1536,1024]{1,0:T(8,128)(2,1)S(1)} %get-tuple-element.63), channel_id=1, source_target_pairs={{2,1},{4,3},{6,5},{8,7},{10,9},{12,11},{14,13},{18,17},{20,19},{22... | collective-permute-start | bytes 9437192 | tf_op jit(solution)/shard_map/cond/branch_1_fun/ppermute | solution.py:232
  61.4 15.5 %collective-permute-start.5 = (f32[12,128]{1,0:T(8,128)S(1)}, f32[12,128]{1,0:T(8,128)S(1)}, u32[]{:S(2)}, u32[]{:S(2)}) collective-permute-start(f32[12,128]{1,0:T(8,128)S(1)} %get-tuple-element.98), channel_id=1, source_target_pairs={{0,1},{1,0},{2,3},{3,2},{4,5},{5,4},{6,7},{7,6},{8,9},{9,8},{10,11... | collective-permute-start | bytes 18440 | tf_op jit(solution)/shard_map/ppermute | solution.py:256
  62.1 14.7 %collective-permute-start.2 = (f32[12,128]{1,0:T(8,128)S(1)}, f32[12,128]{1,0:T(8,128)S(1)}, u32[]{:S(2)}, u32[]{:S(2)}) collective-permute-start(f32[12,128]{1,0:T(8,128)S(1)} %get-tuple-element.76), channel_id=1, source_target_pairs={{1,2},{3,4},{5,6},{7,8},{9,10},{11,12},{13,14},{17,18},{19,20},{21... | collective-permute-start | bytes 18440 | tf_op jit(solution)/shard_map/cond/branch_1_fun/ppermute | solution.py:245
